TPU v7x, 32 devices: a whole 2x2x4 slice. The times are simulated.
32 devices in a mesh: seq: 8 (over z, x), head: 4 (over y, core).
Axes of the slice: x: 2, y: 2, z: 4, core: 2. Of those that a mesh axis runs over, the one named last changes fastest.
Arguments:
- queries: bfloat16 [12288, 4096], P(('seq', 'head')), may hold values from -32 to 32
- cache_keys: bfloat16 [65536, 1024], P('seq', 'head'), may hold values from -12 to 12
- cache_values: bfloat16 [65536, 1024], P('seq', 'head'), may hold values from -6 to 6
- block_ids: int32 [96, 8], P('seq'), may hold values from 0 to 511, as said below
Outputs:
- attention: bfloat16 [12288, 4096], P(('seq', 'head'))
Inputs may be any that keep to these rules, and one draw needn't show every extreme that they name: `block_ids`: entries 0 to 4 of row r name distinct blocks c with c // 64 == r // 12; the other 3 entries name blocks with another value of c // 64, distinct within the row. Among the far entries of the 12 rows with one value of r // 12, at most 6 name blocks of any one other value of c // 64, and exactly 6 do for some value.
All inputs are finite; a program needn't handle non-finite values.
Results may differ from a plain program's by a relative error of at most 0.0043.
Values may be sent and summed in bfloat16 or wider, within the bound.
A program may use at most 128 MiB of HBM per device.

v0:
```python
import math

import jax
import jax.numpy as jnp
from jax import lax
from jax.sharding import PartitionSpec as P

HD = 128
BLK = 128
NEAR = 5


def block_partials(query_rows, key_rows, value_rows):
    score_scale = query_rows.shape[-1] ** (-0.5)
    scores = (
        jnp.einsum("aqgrd,apkgd->apgrqk", query_rows, key_rows, preferred_element_type=jnp.float32)
        * score_scale
    )
    block_max = jnp.max(scores, axis=-1)
    exponent = jnp.exp(scores - block_max[..., None])
    block_sum = jnp.sum(exponent, axis=-1)
    partial_value = jnp.einsum(
        "apgrqk,apkgd->apqgrd",
        exponent.astype(jnp.bfloat16),
        value_rows,
        preferred_element_type=jnp.float32,
    )
    return (partial_value, block_max, block_sum)


def merge_picks(partial_value, block_max, block_sum):
    highest = jnp.max(block_max, axis=-4, keepdims=True)
    factor = jnp.exp(block_max - highest)
    denominator = jnp.sum(factor * block_sum, axis=-4)
    numerator = jnp.sum(partial_value * jnp.moveaxis(factor, -1, -3)[..., None], axis=-5)
    return numerator / jnp.moveaxis(denominator, -1, -3)[..., None]


def slot_places(owner_of, seq_count, capacity):
    owner_hits = (owner_of[:, None] == jnp.arange(seq_count, dtype=jnp.int32)[None, :]).astype(
        jnp.int32
    )
    before = jnp.cumsum(owner_hits, axis=0) - owner_hits
    owner_rank = jnp.sum(before * owner_hits, axis=1)
    return owner_of * capacity + owner_rank


def grouped(array, per_step):
    return array.reshape((array.shape[0] // per_step, per_step) + array.shape[1:])


def shards(queries, cache_keys, cache_values, block_ids):
    seq_count = lax.axis_size("seq")
    seq_place = lax.axis_index("seq")
    by_heads = lax.all_to_all(queries, "head", split_axis=1, concat_axis=0, tiled=True)
    kv_local = cache_keys.shape[1] // HD
    q_width = by_heads.shape[1]
    ratio = q_width // (kv_local * HD)
    q_count = by_heads.shape[0] // BLK
    k_count = cache_keys.shape[0] // BLK
    far_count = block_ids.shape[1] - NEAR
    capacity = max(2, (far_count * q_count + seq_count - 2) // (seq_count - 1))
    slot_total = seq_count * capacity
    per_step = math.gcd(q_count, 4)
    q_blocks = by_heads.reshape(q_count, BLK, kv_local, ratio, HD)
    k_blocks = cache_keys.reshape(k_count, BLK, kv_local, HD)
    v_blocks = cache_values.reshape(k_count, BLK, kv_local, HD)
    near_ids = (block_ids[:, :NEAR] - seq_place * k_count).reshape(-1)
    far_ids = block_ids[:, NEAR:].reshape(-1)
    far_owner = far_ids // k_count
    far_within = far_ids - far_owner * k_count
    far_slot = slot_places(far_owner, seq_count, capacity)
    slot_range = jnp.arange(slot_total, dtype=jnp.int32)
    placed = (far_slot[:, None] == slot_range[None, :]).astype(jnp.int32)
    asked = jnp.sum(placed * far_within[:, None], axis=0).reshape(seq_count, capacity)
    wanted = lax.all_to_all(asked, "seq", split_axis=0, concat_axis=0, tiled=True)
    wanted_flat = wanted.reshape(-1)
    near_k = jnp.take(k_blocks, near_ids, axis=0).reshape(q_count, NEAR, BLK, kv_local, HD)
    near_v = jnp.take(v_blocks, near_ids, axis=0).reshape(q_count, NEAR, BLK, kv_local, HD)
    sent_k = jnp.take(k_blocks, wanted_flat, axis=0).reshape(
        seq_count, capacity, BLK, kv_local * HD
    )
    sent_v = jnp.take(v_blocks, wanted_flat, axis=0).reshape(
        seq_count, capacity, BLK, kv_local * HD
    )
    got_k, got_v = (
        lax.all_to_all(sent_k, "seq", split_axis=0, concat_axis=0, tiled=True),
        lax.all_to_all(sent_v, "seq", split_axis=0, concat_axis=0, tiled=True),
    )
    far_k = jnp.take(got_k.reshape(slot_total, BLK, kv_local, HD), far_slot, axis=0).reshape(
        q_count, far_count, BLK, kv_local, HD
    )
    far_v = jnp.take(got_v.reshape(slot_total, BLK, kv_local, HD), far_slot, axis=0).reshape(
        q_count, far_count, BLK, kv_local, HD
    )
    all_k = jnp.concatenate([near_k, far_k], axis=1)
    all_v = jnp.concatenate([near_v, far_v], axis=1)

    def attend(pieces):
        return merge_picks(*block_partials(*pieces)).astype(jnp.bfloat16)

    result = lax.map(
        attend, (grouped(q_blocks, per_step), grouped(all_k, per_step), grouped(all_v, per_step))
    )
    result = result.reshape(q_count * BLK, q_width)
    return lax.all_to_all(result, "head", split_axis=0, concat_axis=1, tiled=True)


def solution(mesh):
    return jax.shard_map(
        shards,
        mesh=mesh,
        in_specs=(P(("seq", "head"), None), P("seq", "head"), P("seq", "head"), P("seq", None)),
        out_specs=P(("seq", "head"), None),
        check_vma=False,
    )
```

profile of v0, /device:TPU:10, one launch (start us, length us, event | category | flops | bytes accessed | tf_op | source)
XLA Modules:
  0.0 354.6 jit_solution(16657429014959150892)
XLA Ops:
  2.0 6.2 %all-to-all-start = ((s32[8,1,6]{2,1,0:T(1,128)}), s32[8,1,6]{2,1,0:T(1,128)S(1)}, u32[]{:S(2)}, u32[]{:S(2)}) async-start(s32[8,1,6]{2,1,0:T(1,128)} %bitcast.16), calls=%async_computation | async-start | bytes 8192 | tf_op jit(solution)/shard_map/all_to_all | solution.py:76
  16.0 6.9 %reshape.221 = bf16[64,128,2,128]{3,2,1,0:T(2,128)(2,1)} reshape(bf16[8192,256]{1,0:T(8,128)(2,1)} %param.13) | data formatting | bytes 8388608 | tf_op jit(solution)/shard_map/reshape | solution.py:66
  22.9 5.4 %copy.130 = bf16[64,128,2,128]{3,1,2,0:T(8,128)(2,1)} copy(bf16[64,128,2,128]{3,2,1,0:T(2,128)(2,1)} %reshape.221) | data formatting | bytes 8388608 | tf_op jit(solution)/shard_map/reshape | solution.py:66
  28.3 6.9 %reshape.220 = bf16[64,128,2,128]{3,2,1,0:T(2,128)(2,1)} reshape(bf16[8192,256]{1,0:T(8,128)(2,1)} %param.14) | data formatting | bytes 8388608 | tf_op jit(solution)/shard_map/reshape | solution.py:67
  35.2 5.3 %copy.121 = bf16[64,128,2,128]{3,1,2,0:T(8,128)(2,1)} copy(bf16[64,128,2,128]{3,2,1,0:T(2,128)(2,1)} %reshape.220) | data formatting | bytes 8388608 | tf_op jit(solution)/shard_map/reshape | solution.py:67
  41.8 4.9 %gather_fusion.4 = bf16[48,128,2,128]{3,1,2,0:T(8,128)(2,1)} fusion(bf16[64,128,2,128]{3,1,2,0:T(8,128)(2,1)} %copy.130, s32[1024]{0:T(1024)S(1)} %pad_clamp_fusion.1), kind=kCustom, calls=%fused_computation.4.clone | custom fusion | bytes 6291648 | tf_op jit(solution)/shard_map/jit(_take)/gather | solution.py:80
  51.5 6.1 %broadcast_select_fusion.2 = (bf16[48,128,2,128]{3,1,2,0:T(8,128)(2,1)}, bf16[48,128,2,128]{3,1,2,0:T(8,128)(2,1)}) fusion(bf16[48,128,2,128]{3,1,2,0:T(8,128)(2,1)} %gather_fusion.4, pred[48]{0:T(512)(128)(4,1)S(1)} %compare_and_fusion.1, bf16[48,128,2,128]{3,1,2,0:T(8,128)(2,1)} %gather_fusion.1), kind=kLoop, calls=%fused_computation.34 | loop fusion | flops 3145728 | bytes 12582960 | tf_op jit(solution)/shard_map/jit(_take)/select_n | solution.py:80
  62.4 6.7 %all-to-all-start.2 = ((bf16[8,6,128,256]{2,3,1,0:T(8,128)(2,1)}), bf16[8,6,128,256]{2,3,1,0:T(8,128)(2,1)}, u32[]{:S(2)}, u32[]{:S(2)}) async-start(bf16[8,6,128,256]{2,3,1,0:T(8,128)(2,1)} %bitcast.90), calls=%async_computation.2 | async-start | bytes 6291456 | tf_op jit(solution)/shard_map/all_to_all | solution.py:87
  73.8 63.7 %all-to-all-done.2 = bf16[8,6,128,256]{2,3,1,0:T(8,128)(2,1)} async-done(((bf16[8,6,128,256]{2,3,1,0:T(8,128)(2,1)}), bf16[8,6,128,256]{2,3,1,0:T(8,128)(2,1)}, u32[]{:S(2)}, u32[]{:S(2)}) %all-to-all-start.2) | async-done | bytes 3145760 | tf_op jit(solution)/shard_map/all_to_all | solution.py:87
  137.4 7.9 %all-to-all-start.1 = ((bf16[8,6,128,256]{2,3,1,0:T(8,128)(2,1)}), bf16[8,6,128,256]{2,3,1,0:T(8,128)(2,1)}, u32[]{:S(2)}, u32[]{:S(2)}) async-start(bf16[8,6,128,256]{2,3,1,0:T(8,128)(2,1)} %bitcast.88), calls=%async_computation.1 | async-start | bytes 6291456 | tf_op jit(solution)/shard_map/all_to_all | solution.py:88
  145.5 5.2 %gather_fusion = bf16[60,128,2,128]{3,1,2,0:T(8,128)(2,1)} fusion(bf16[64,128,2,128]{3,1,2,0:T(8,128)(2,1)} %copy.121, s32[1024]{0:T(1024)S(1)} %pad_clamp_fusion.2), kind=kCustom, calls=%fused_computation.clone | custom fusion | bytes 7864560 | tf_op jit(solution)/shard_map/jit(_take)/gather | solution.py:79
  150.7 5.2 %gather_fusion.3 = bf16[60,128,2,128]{3,1,2,0:T(8,128)(2,1)} fusion(bf16[64,128,2,128]{3,1,2,0:T(8,128)(2,1)} %copy.130, s32[1024]{0:T(1024)S(1)} %pad_clamp_fusion.2), kind=kCustom, calls=%fused_computation.3.clone | custom fusion | bytes 7864560 | tf_op jit(solution)/shard_map/jit(_take)/gather | solution.py:78
  155.9 5.8 %broadcast_select_fusion = (bf16[60,128,2,128]{3,1,2,0:T(8,128)(2,1)}, bf16[60,128,2,128]{3,1,2,0:T(8,128)(2,1)}) fusion(bf16[60,128,2,128]{3,1,2,0:T(8,128)(2,1)} %gather_fusion.3, pred[60]{0:T(512)(128)(4,1)S(1)} %compare_and_fusion.2, bf16[60,128,2,128]{3,1,2,0:T(8,128)(2,1)} %gather_fusion), kind=kLoop, calls=%fused_computation.31 | loop fusion | flops 3932160 | bytes 15728700 | tf_op jit(solution)/shard_map/jit(_take)/select_n | solution.py:78
  161.7 6.3 %copy.127 = bf16[3,4,5,128,2,128]{3,5,4,2,1,0:T(8,128)(2,1)} copy(bf16[3,4,5,128,2,128]{5,3,4,2,1,0:T(8,128)(2,1)} %bitcast.86) | data formatting | bytes 7864320 | tf_op jit(solution)/shard_map/concatenate | solution.py:97
  175.4 37.5 %all-to-all-done.1 = bf16[8,6,128,256]{2,3,1,0:T(8,128)(2,1)} async-done(((bf16[8,6,128,256]{2,3,1,0:T(8,128)(2,1)}), bf16[8,6,128,256]{2,3,1,0:T(8,128)(2,1)}, u32[]{:S(2)}, u32[]{:S(2)}) %all-to-all-start.1) | async-done | bytes 3145760 | tf_op jit(solution)/shard_map/all_to_all | solution.py:88
  231.9 6.1 %pad_maximum_fusion.1 = bf16[3,4,8,128,2,128]{5,3,4,2,1,0:T(8,128)(2,1)} fusion(bf16[3,4,3,128,2,128]{5,3,4,2,1,0:T(8,128)(2,1)} %bitcast.93, bf16[3,4,5,128,2,128]{5,3,4,2,1,0:T(8,128)(2,1)} %bitcast.85), kind=kLoop, calls=%fused_computation.30 | loop fusion | flops 3145728 | bytes 12582912 | tf_op jit(solution)/shard_map/concatenate | solution.py:96
  241.3 62.1 %while.10 = (s32[]{:T(128)}, bf16[3,4,128,2,4,128]{5,4,3,2,1,0:T(4,128)(2,1)}, bf16[3,4,8,128,2,128]{3,5,4,2,1,0:T(8,128)(2,1)}, bf16[3,4,8,128,2,128]{5,3,4,2,1...) while((s32[]{:T(128)}, bf16[3,4,128,2,4,128]{5,4,3,2,1,0:T(4,128)(2,1)}, ...), condition=%wide.region_9.13_spmd, body=%wide.region_3.12_spmd.sunk | while | flops 2185814016 | bytes 67978824 | solution.py:102
  246.7 5.4 %fusion.26 = (f32[4,8,2,4,128]{4,3,1,2,0:T(4,128)S(1)}, f32[4,2,4,128]{3,2,1,0:T(4,128)S(1)}, bf16[4,8,2,4,128,128]{4,5,3,1,2,0:T(8,128)(2,1)S(1)}) fusion(f32[4,2,8,128,128,4]{4,3,5,2,1,0:T(8,128)S(1)} %get-tuple-element.132, f32[4,8,2,4,128]{4,3,1,2,0:T(4,128)S(1)} %get-tuple-element.133), kind=kLoop, calls=%fused_computation.12.clone.1 | loop fusion | flops 20934656 | bytes 25444352 | tf_op jit(solution)/shard_map/while/body/eval_jaxpr/reduce_sum | solution.py:21
  252.2 5.9 %fusion.27 = f32[4,128,2,4,128]{1,4,3,2,0:T(8,128)} fusion(bf16[4,8,2,4,128,128]{4,5,3,1,2,0:T(8,128)(2,1)S(1)} %get-tuple-element.134, bf16[3,4,8,128,2,128]{3,5,4,2,1,0:T(8,128)(2,1)} %get-tuple-element.151, s32[]{:T(128)} %get-tuple-element.143, f32[4,8,2,4,128]{4,3,1,2,0:T(4,128)S(1)} %get-tuple-element.133, f32[4,128,2,4]{1,3,2,0:T(4,128)S(1)} %bitcast.96), kind=kOutput, calls=%fused_computation.7.clone.1 | convolution fusion | flops 1081638912 | bytes 12730880 | tf_op jit(solution)/shard_map/while/body/eval_jaxpr/apgrqk,apkgd->apqgrd/dot_general | solution.py:22
  267.4 5.4 %fusion.26 = (f32[4,8,2,4,128]{4,3,1,2,0:T(4,128)S(1)}, f32[4,2,4,128]{3,2,1,0:T(4,128)S(1)}, bf16[4,8,2,4,128,128]{4,5,3,1,2,0:T(8,128)(2,1)S(1)}) fusion(f32[4,2,8,128,128,4]{4,3,5,2,1,0:T(8,128)S(1)} %get-tuple-element.132, f32[4,8,2,4,128]{4,3,1,2,0:T(4,128)S(1)} %get-tuple-element.133), kind=kLoop, calls=%fused_computation.12.clone.1 | loop fusion | flops 20934656 | bytes 25444352 | tf_op jit(solution)/shard_map/while/body/eval_jaxpr/reduce_sum | solution.py:21
  272.9 5.9 %fusion.27 = f32[4,128,2,4,128]{1,4,3,2,0:T(8,128)} fusion(bf16[4,8,2,4,128,128]{4,5,3,1,2,0:T(8,128)(2,1)S(1)} %get-tuple-element.134, bf16[3,4,8,128,2,128]{3,5,4,2,1,0:T(8,128)(2,1)} %get-tuple-element.151, s32[]{:T(128)} %get-tuple-element.143, f32[4,8,2,4,128]{4,3,1,2,0:T(4,128)S(1)} %get-tuple-element.133, f32[4,128,2,4]{1,3,2,0:T(4,128)S(1)} %bitcast.96), kind=kOutput, calls=%fused_computation.7.clone.1 | convolution fusion | flops 1081638912 | bytes 12730880 | tf_op jit(solution)/shard_map/while/body/eval_jaxpr/apgrqk,apkgd->apqgrd/dot_general | solution.py:22
  288.1 5.4 %fusion.26 = (f32[4,8,2,4,128]{4,3,1,2,0:T(4,128)S(1)}, f32[4,2,4,128]{3,2,1,0:T(4,128)S(1)}, bf16[4,8,2,4,128,128]{4,5,3,1,2,0:T(8,128)(2,1)S(1)}) fusion(f32[4,2,8,128,128,4]{4,3,5,2,1,0:T(8,128)S(1)} %get-tuple-element.132, f32[4,8,2,4,128]{4,3,1,2,0:T(4,128)S(1)} %get-tuple-element.133), kind=kLoop, calls=%fused_computation.12.clone.1 | loop fusion | flops 20934656 | bytes 25444352 | tf_op jit(solution)/shard_map/while/body/eval_jaxpr/reduce_sum | solution.py:21
  293.6 5.9 %fusion.27 = f32[4,128,2,4,128]{1,4,3,2,0:T(8,128)} fusion(bf16[4,8,2,4,128,128]{4,5,3,1,2,0:T(8,128)(2,1)S(1)} %get-tuple-element.134, bf16[3,4,8,128,2,128]{3,5,4,2,1,0:T(8,128)(2,1)} %get-tuple-element.151, s32[]{:T(128)} %get-tuple-element.143, f32[4,8,2,4,128]{4,3,1,2,0:T(4,128)S(1)} %get-tuple-element.133, f32[4,128,2,4]{1,3,2,0:T(4,128)S(1)} %bitcast.96), kind=kOutput, calls=%fused_computation.7.clone.1 | convolution fusion | flops 1081638912 | bytes 12730880 | tf_op jit(solution)/shard_map/while/body/eval_jaxpr/apgrqk,apkgd->apqgrd/dot_general | solution.py:22
  308.0 40.3 %all_to_all.54 = bf16[4,384,1024]{2,1,0:T(8,128)(2,1)} all-to-all(bf16[4,384,1024]{2,1,0:T(8,128)(2,1)S(1)} %all_to_all.45), channel_id=1, replica_groups=mesh['seq'=8,'head'=4] {'head'}, dimensions={0} | all-to-all | bytes 6291456 | tf_op jit(solution)/shard_map/all_to_all | solution.py:106
  (67 shorter events, 94.3 us)
Async XLA Ops:
  2.0 10.3 %all-to-all-start = ((s32[8,1,6]{2,1,0:T(1,128)}), s32[8,1,6]{2,1,0:T(1,128)S(1)}, u32[]{:S(2)}, u32[]{:S(2)}) async-start(s32[8,1,6]{2,1,0:T(1,128)} %bitcast.16), calls=%async_computation | async-start | bytes 8192 | tf_op jit(solution)/shard_map/all_to_all | solution.py:76
  12.3 50.1 %all-to-all-start.3 = ((bf16[384,4,1024]{2,0,1:T(8,128)(2,1)}), bf16[384,4,1024]{2,0,1:T(8,128)(2,1)S(1)}, u32[]{:S(2)}, u32[]{:S(2)}) async-start(bf16[384,4,1024]{2,0,1:T(8,128)(2,1)} %bitcast.89), calls=%async_computation.3 | async-start | bytes 6291456 | tf_op jit(solution)/shard_map/all_to_all | solution.py:55
  62.4 75.0 %all-to-all-start.2 = ((bf16[8,6,128,256]{2,3,1,0:T(8,128)(2,1)}), bf16[8,6,128,256]{2,3,1,0:T(8,128)(2,1)}, u32[]{:S(2)}, u32[]{:S(2)}) async-start(bf16[8,6,128,256]{2,3,1,0:T(8,128)(2,1)} %bitcast.90), calls=%async_computation.2 | async-start | bytes 6291456 | tf_op jit(solution)/shard_map/all_to_all | solution.py:87
  137.4 7.9 %copy-start.2 = (s32[12,8]{0,1:T(8,128)S(1)}, s32[12,8]{0,1:T(8,128)}, u32[]{:S(2)}) copy-start(s32[12,8]{0,1:T(8,128)} %param.15) | copy-start | bytes 1156
  137.4 75.4 %all-to-all-start.1 = ((bf16[8,6,128,256]{2,3,1,0:T(8,128)(2,1)}), bf16[8,6,128,256]{2,3,1,0:T(8,128)(2,1)}, u32[]{:S(2)}, u32[]{:S(2)}) async-start(bf16[8,6,128,256]{2,3,1,0:T(8,128)(2,1)} %bitcast.88), calls=%async_computation.1 | async-start | bytes 6291456 | tf_op jit(solution)/shard_map/all_to_all | solution.py:88
  219.9 4.6 %copy-start.1 = (bf16[36,128,2,128]{3,1,2,0:T(8,128)(2,1)S(1)}, bf16[36,128,2,128]{3,1,2,0:T(8,128)(2,1)}, u32[]{:S(2)}) copy-start(bf16[36,128,2,128]{3,1,2,0:T(8,128)(2,1)} %gather_fusion.5) | copy-start | bytes 7077892
  231.9 6.1 %copy-start = (bf16[3,4,5,128,2,128]{3,5,4,2,1,0:T(8,128)(2,1)S(1)}, bf16[3,4,5,128,2,128]{3,5,4,2,1,0:T(8,128)(2,1)}, u32[]{:S(2)}) copy-start(bf16[3,4,5,128,2,128]{3,5,4,2,1,0:T(8,128)(2,1)} %copy.127) | copy-start | bytes 11796484
where the time goes:
time: 361 us; the launch traced here: 355 us
  local copies, waits for them, and re-layouts  111 us (31%)
  waiting for transfers between devices  101 us (28%)
  other arithmetic  48.7 us (13%)
  blocking collectives  40.3 us (11%)
  matrix products  29.1 us (8%)
  starting transfers between devices  24.5 us (7%)
    all_to_all x1, waiting for transfers between devices, shards(): lax.all_to_all(sent_k, 'seq', split_axis=0, concat_axis=0, tiled=True)  63.7 us
    all_to_all x1, blocking collectives, shards(): lax.all_to_all(result, 'head', split_axis=0, concat_axis=1, tiled=True)  40.3 us
    all_to_all x1, waiting for transfers between devices, shards(): lax.all_to_all(sent_v, 'seq', split_axis=0, concat_axis=0, tiled=True)  37.5 us
    dot_general x3, matrix products, block_partials(): jnp.einsum('apgrqk,apkgd->apqgrd', exponent.astype(jnp.bfloat16), value_r...  17.6 us
    reduce_sum x3, other arithmetic, block_partials(): block_sum = jnp.sum(exponent, axis=-1)  16.1 us
    reshape x2, local copies, waits for them, and re-layouts, shards(): k_blocks = cache_keys.reshape(k_count, BLK, kv_local, HD)  12.3 us
    reshape x2, local copies, waits for them, and re-layouts, shards(): v_blocks = cache_values.reshape(k_count, BLK, kv_local, HD)  12.2 us
    dot_general x3, matrix products, block_partials(): jnp.einsum('aqgrd,apkgd->apgrqk', query_rows, key_rows, preferred_element...  11.5 us
  transfers between devices with their start and end apart: 4, of which 3 were waited for; matrix products, arithmetic and copies ran while one was open for 24% of the time, Pallas kernels for 0%

commit v1 on v0

v1 whole, which is shorter than its diff:
```python
import functools
import math

import jax
import jax.numpy as jnp
from jax import lax
from jax.experimental import pallas as pl
from jax.experimental.pallas import tpu as pltpu
from jax.sharding import PartitionSpec as P

HD = 128
BLK = 128
NEAR = 5
MESH = pl.DeviceIdType.MESH
LOG2E = math.log2(math.e)


def aligned(index, size):
    return pl.ds(pl.multiple_of(index * size, size), size)


def kernel(
    seq_count, head_count, capacity, kv_local, ratio, per_head, far_count,
    ids, asked, queries, keys, values, out,
    k_buf, v_buf, q_buf, got, wanted, send_bufs, recv_bufs, stage,
    id_send, id_recv, q_send, q_recv, f_send, f_recv, o_send, o_recv, o_local, local,
):
    seq = lax.axis_index("seq")
    head = lax.axis_index("head")
    others = seq_count - 1
    rows = queries.shape[0]
    q_width = q_buf.shape[1]
    width = ratio * HD

    def head_peer(step):
        return (head // 2 + step // 2) % 2 * 2 + (head % 2 + step % 2) % 2

    k_load = pltpu.make_async_copy(keys, k_buf, local.at[0])
    v_load = pltpu.make_async_copy(values, v_buf, local.at[1])
    q_own = pltpu.make_async_copy(
        queries.at[:, aligned(head, q_width)], q_buf.at[aligned(head, rows)], local.at[2]
    )
    k_load.start()
    v_load.start()
    q_own.start()

    barrier = pltpu.get_barrier_semaphore()
    for step in range(1, seq_count):
        pl.semaphore_signal(
            barrier, inc=1, device_id={"seq": (seq + step) % seq_count}, device_id_type=MESH
        )
    for step in range(1, head_count):
        pl.semaphore_signal(
            barrier, inc=1, device_id={"head": head_peer(step)}, device_id_type=MESH
        )
    pl.semaphore_wait(barrier, others + head_count - 1)

    def id_copy(step):
        return pltpu.make_async_remote_copy(
            src_ref=asked.at[step],
            dst_ref=got.at[step],
            send_sem=id_send.at[step],
            recv_sem=id_recv.at[step],
            device_id={"seq": (seq + seq_count - 1 - step) % seq_count},
            device_id_type=MESH,
        )

    def q_copy(step):
        peer = head_peer(step)
        return pltpu.make_async_remote_copy(
            src_ref=queries.at[:, aligned(peer, q_width)],
            dst_ref=q_buf.at[aligned(head, rows)],
            send_sem=q_send.at[step - 1],
            recv_sem=q_recv.at[step - 1],
            device_id={"head": peer},
            device_id_type=MESH,
        )

    def far_copy(g, step):
        block = pl.ds(step * capacity, capacity)
        return pltpu.make_async_remote_copy(
            src_ref=send_bufs[g].at[block],
            dst_ref=recv_bufs[g].at[block],
            send_sem=f_send.at[g, step],
            recv_sem=f_recv.at[g, step],
            device_id={"seq": (seq + 1 + step) % seq_count},
            device_id_type=MESH,
        )

    def out_copy(g, step, j):
        peer = head_peer(step)
        return pltpu.make_async_remote_copy(
            src_ref=stage.at[g, peer * per_head + j],
            dst_ref=out.at[aligned(j, BLK), pl.ds(pl.multiple_of(head * q_width + g * width, width), width)],
            send_sem=o_send.at[g, step - 1, j],
            recv_sem=o_recv.at[g, step - 1, j],
            device_id={"head": peer},
            device_id_type=MESH,
        )

    def own_copy(g, j):
        return pltpu.make_async_copy(
            stage.at[g, head * per_head + j],
            out.at[aligned(j, BLK), pl.ds(pl.multiple_of(head * q_width + g * width, width), width)],
            o_local.at[g, j],
        )

    for step in range(others):
        id_copy(step).start()
    for step in range(head_count - 1, 0, -1):
        q_copy(step).start()
    for step in range(others):
        id_copy(step).wait_recv()
    to_scalar = pltpu.make_async_copy(got, wanted, local.at[3])
    to_scalar.start()
    to_scalar.wait()
    k_load.wait()
    v_load.wait()

    def gather(g, step):
        columns = slice(g * HD, (g + 1) * HD)
        for slot in range(capacity):
            block = wanted[step, 0, slot]
            place = step * capacity + slot
            send_bufs[g][place, :, 0:HD] = k_buf[block, :, columns]
            send_bufs[g][place, :, HD:] = v_buf[block, :, columns]

    @pl.loop(0, others)
    def _(step):
        gather(0, step)
        far_copy(0, step).start()

    for g in range(1, kv_local):
        @pl.loop(0, others)
        def _(step):
            gather(g, step)

        @pl.loop(0, others)
        def _(step):
            far_copy(g - 1, step).wait_send()
            far_copy(g, step).start()

    q_own.wait()
    for step in range(1, head_count):
        q_copy(step).wait_recv()

    def attend(g, b):
        columns = slice(g * HD, (g + 1) * HD)
        near = [ids[b, j] for j in range(NEAR)]
        far = [ids[b, NEAR + j] for j in range(far_count)]
        k_all = jnp.concatenate(
            [k_buf[block, :, columns] for block in near]
            + [recv_bufs[g][block, :, 0:HD] for block in far], axis=0
        )
        v_all = jnp.concatenate(
            [v_buf[block, :, columns] for block in near]
            + [recv_bufs[g][block, :, HD:] for block in far], axis=0
        )
        q_rows = q_buf[aligned(b, BLK), g * width:(g + 1) * width]
        pair = 2 if ratio % 2 == 0 else 1
        for first in range(0, ratio, pair):
            q_part = jnp.concatenate(
                [q_rows[:, r * HD:(r + 1) * HD] for r in range(first, first + pair)], axis=0
            )
            scores = lax.dot_general(
                q_part, k_all, (((1,), (1,)), ((), ())), preferred_element_type=jnp.float32
            )
            highest = jnp.max(scores, axis=1, keepdims=True)
            exponent = jnp.exp2((scores - highest) * (HD ** -0.5 * LOG2E))
            total = jnp.sum(exponent, axis=1, keepdims=True)
            mixed = jnp.dot(
                exponent.astype(jnp.bfloat16), v_all, preferred_element_type=jnp.float32
            )
            result = (mixed / total).astype(jnp.bfloat16)
            for r in range(pair):
                stage[g, b, :, (first + r) * HD:(first + r + 1) * HD] = (
                    result[r * BLK:(r + 1) * BLK]
                )

    for g in range(kv_local):
        @pl.loop(0, others)
        def _(step):
            far_copy(g, step).wait_recv()

        @pl.loop(0, (head_count - 1) * per_head)
        def _(index):
            step = head_count - 1 - index // per_head
            j = index % per_head
            attend(g, head_peer(step) * per_head + j)
            out_copy(g, step, j).start()

        @pl.loop(0, per_head)
        def _(j):
            attend(g, head * per_head + j)
            own_copy(g, j).start()

    for step in range(others):
        id_copy(step).wait_send()
        far_copy(kv_local - 1, step).wait_send()
    for step in range(1, head_count):
        q_copy(step).wait_send()
    for g in range(kv_local):
        @pl.loop(0, (head_count - 1) * per_head)
        def _(index):
            step = head_count - 1 - index // per_head
            j = index % per_head
            out_copy(g, step, j).wait()

        @pl.loop(0, per_head)
        def _(j):
            own_copy(g, j).wait()


def shards(queries, cache_keys, cache_values, block_ids):
    seq_count = lax.axis_size("seq")
    head_count = lax.axis_size("head")
    seq = lax.axis_index("seq")
    rows, q_columns = queries.shape
    q_width = q_columns // head_count
    kv_local = cache_keys.shape[1] // HD
    ratio = q_width // (kv_local * HD)
    q_count, picks = block_ids.shape
    per_head = q_count // head_count
    k_count = cache_keys.shape[0] // BLK
    far_count = picks - NEAR
    others = seq_count - 1
    capacity = max(2, (far_count * q_count + seq_count - 2) // others)

    near = block_ids[:, :NEAR] - seq * k_count
    far = block_ids[:, NEAR:].reshape(-1)
    owner = far // k_count
    within = far - owner * k_count
    distance = (seq - owner + seq_count) % seq_count - 1
    order = jnp.arange(far.shape[0], dtype=jnp.int32)
    earlier = (distance[:, None] == distance[None, :]) & (order[None, :] < order[:, None])
    rank = jnp.sum(earlier.astype(jnp.int32), axis=1)
    slot = distance * capacity + rank
    ids = jnp.concatenate([near, slot.reshape(q_count, far_count)], axis=1)
    lane = jnp.arange(128, dtype=jnp.int32)[None, None, None, :]
    shape = (far.shape[0], others, 8, 128)
    hit = (
        (distance[:, None, None, None] == jnp.arange(others, dtype=jnp.int32)[None, :, None, None])
        & (rank[:, None, None, None] == lane)
    )
    asked = jnp.sum(
        jnp.where(jnp.broadcast_to(hit, shape), within[:, None, None, None], 0), axis=0
    )

    slots = others * capacity
    blocks = (k_count, BLK, cache_keys.shape[1])
    bf16 = jnp.bfloat16
    dma = pltpu.SemaphoreType.DMA
    anywhere = pl.BlockSpec(memory_space=pl.ANY)
    return pl.pallas_call(
        functools.partial(
            kernel, seq_count, head_count, capacity, kv_local, ratio, per_head, far_count
        ),
        out_shape=jax.ShapeDtypeStruct((rows, q_columns), bf16),
        in_specs=[
            pl.BlockSpec(memory_space=pltpu.SMEM),
            pl.BlockSpec(memory_space=pltpu.VMEM),
            anywhere, anywhere, anywhere,
        ],
        out_specs=anywhere,
        scratch_shapes=[
            pltpu.VMEM(blocks, bf16),
            pltpu.VMEM(blocks, bf16),
            pltpu.VMEM((rows * head_count, q_width), bf16),
            pltpu.VMEM((others, 8, 128), jnp.int32),
            pltpu.SMEM((others, 8, 128), jnp.int32),
            [pltpu.VMEM((slots, BLK, 2 * HD), bf16) for _ in range(kv_local)],
            [pltpu.VMEM((slots, BLK, 2 * HD), bf16) for _ in range(kv_local)],
            pltpu.VMEM((kv_local, q_count, BLK, ratio * HD), bf16),
            dma((others,)), dma((others,)),
            dma((head_count - 1,)), dma((head_count - 1,)),
            dma((kv_local, others)), dma((kv_local, others)),
            dma((kv_local, head_count - 1, per_head)),
            dma((kv_local, head_count - 1, per_head)),
            dma((kv_local, per_head)),
            dma((4,)),
        ],
        compiler_params=pltpu.CompilerParams(
            collective_id=0, has_side_effects=True, vmem_limit_bytes=56 * 2**20
        ),
    )(ids, asked, queries, cache_keys.reshape(blocks), cache_values.reshape(blocks))


def solution(mesh):
    return jax.shard_map(
        shards,
        mesh=mesh,
        in_specs=(P(("seq", "head"), None), P("seq", "head"), P("seq", "head"), P("seq", None)),
        out_specs=P(("seq", "head"), None),
        check_vma=False,
    )
```

time: 361 us -> 173 us (0.48); the launches traced: 355 us -> 173 us
  Pallas kernels: 0 us -> 165 us
  local copies, waits for them, and re-layouts: 111 us -> 5.63 us
  waiting for transfers between devices: 101 us -> 0 us
  other arithmetic: 48.7 us -> 1.97 us
  blocking collectives: 40.3 us -> 0 us
  matrix products: 29.1 us -> 0 us
  starting transfers between devices: 24.5 us -> 0 us
    pallas_call x0 -> x1, Pallas kernels: none -> 165 us  [shards(): pl.pallas_call(functools.partial(kernel, seq_count, head_count, capacity,...]
    all_to_all x4 -> x0, waiting for transfers between devices: 101 us -> none  [the longest x1 63.7 us: shards(): lax.all_to_all(sent_k, 'seq', split_axis=0, concat_axis=0, tiled=True)]
    all_to_all x1 -> x0, blocking collectives: 40.3 us -> none  [shards(): lax.all_to_all(result, 'head', split_axis=0, concat_axis=1, tiled=True)]
    reshape x9 -> x1, local copies, waits for them, and re-layouts: 32.9 us -> 0.08 us  [shards(): far = block_ids[:, NEAR:].reshape(-1)]
    dot_general x6 -> x0, matrix products: 29.1 us -> none  [the longest x3 17.6 us: block_partials(): jnp.einsum('apgrqk,apkgd->apqgrd', exponent.astype(jnp.bfloat16), value_r...]
    gather x6 -> x0, local copies, waits for them, and re-layouts: 27.1 us -> none  [the longest x1 5.2 us: shards(): jnp.take(v_blocks, near_ids, axis=0)]
    all_to_all x4 -> x0, starting transfers between devices: 24.5 us -> none  [the longest x1 7.86 us: shards(): lax.all_to_all(sent_v, 'seq', split_axis=0, concat_axis=0, tiled=True)]
    select_n x6 -> x0, other arithmetic: 16.4 us -> none  [the longest x1 6.15 us: shards(): jnp.take(k_blocks, wanted_flat, axis=0)]
  transfers between devices with their start and end apart: 4 -> 0, of which waited for: 3 -> 0; matrix products, arithmetic and copies ran while one was open for 24% -> 0% of each run, Pallas kernels for 0% -> 0%
where the time goes in v1:
time: 173 us
  Pallas kernels  165 us (95%)
  local copies, waits for them, and re-layouts  5.63 us (3%)
  other arithmetic  1.97 us (1%)
    pallas_call x1, Pallas kernels, shards(): pl.pallas_call(functools.partial(kernel, seq_count, head_count, capacity,...  165 us
    unnamed x3, local copies, waits for them, and re-layouts  4.78 us

profile of v1, /device:TPU:10, one launch (start us, length us, event | category | flops | bytes accessed | tf_op | source)
XLA Modules:
  0.0 173.0 jit_solution(17009954386213057842)
XLA Ops:
  0.0 0.7 slice.7
  0.7 0.1 copy.12
  0.8 0.1 reshape.202
  0.9 0.2 convert_reduce_fusion
  1.1 0.1 iota_compare_fusion.1
  1.2 0.1 iota_compare_fusion
  1.2 0.1 reduce_sum.21
  1.4 0.8 copy.11
  2.1 0.7 pad_add_fusion.ids
  2.8 0.1 broadcast_and_fusion
  2.9 0.8 select_reduce_fusion.asked
  3.7 165.4 %shard_map.46 = bf16[384,4096]{1,0:T(8,128)(2,1)} custom-call(s32[12,8]{1,0:T(8,128)} %pad_add_fusion.ids, s32[7,8,128]{2,1,0:T(8,128)} %select_reduce_fusion.asked, bf16[384,4096]{1,0:T(8,128)(2,1)} %queries.1, bf16[64,128,256]{2,1,0:T(8,128)(2,1)} %bitcast.3, bf16[64,128,256]{2,1,0:T(8,128)(2,1)} %bitcast.4), custom_call_target="tpu_custom_call" | custom-call | tf_op jit(solution)/shard_map/pallas_call | solution.py:254
  169.1 3.9 %copy.14 = bf16[384,4096]{1,0:T(8,128)(2,1)} copy(bf16[384,4096]{1,0:T(8,128)(2,1)} %shard_map.46) | data formatting | bytes 6291456
  (4 shorter events, 0.1 us)

commit v2 on v1

--- a/solution.py
+++ b/solution.py
@@ -23,7 +23,7 @@
     seq_count, head_count, capacity, kv_local, ratio, per_head, far_count,
     ids, asked, queries, keys, values, out,
     k_buf, v_buf, q_buf, got, wanted, send_bufs, recv_bufs, stage,
-    id_send, id_recv, q_send, q_recv, f_send, f_recv, o_send, o_recv, o_local, local,
+    id_send, id_recv, q_send, q_recv, f_send, f_recv, o_send, o_recv, o_local, local, turn, near_mixed, near_high, near_total,
 ):
     seq = lax.axis_index("seq")
     head = lax.axis_index("head")
@@ -125,50 +125,107 @@
             send_bufs[g][place, :, 0:HD] = k_buf[block, :, columns]
             send_bufs[g][place, :, HD:] = v_buf[block, :, columns]
 
-    @pl.loop(0, others)
-    def _(step):
-        gather(0, step)
-        far_copy(0, step).start()
+    core = head % 2
+
+    @pl.when(core == 0)
+    def _():
+        @pl.loop(0, others)
+        def _(step):
+            gather(0, step)
+            far_copy(0, step).start()
+
+    @pl.when(core == 1)
+    def _():
+        @pl.loop(0, others)
+        def _(step):
+            gather(0, step)
 
     for g in range(1, kv_local):
         @pl.loop(0, others)
         def _(step):
             gather(g, step)
 
-        @pl.loop(0, others)
-        def _(step):
-            far_copy(g - 1, step).wait_send()
-            far_copy(g, step).start()
+    def advance(g):
+        @pl.loop(0, others)
+        def _(step):
+            far_copy(g, step).wait_send()
+            if g + 1 < kv_local:
+                far_copy(g + 1, step).start()
+
+    @pl.when(core == 0)
+    def _():
+        @pl.loop(0, others)
+        def _(step):
+            far_copy(0, step).wait_send()
+            pl.semaphore_signal(
+                turn.at[step], inc=1, device_id={"head": head_peer(1)}, device_id_type=MESH
+            )
+            if kv_local > 1:
+                far_copy(1, step).start()
+
+    @pl.when(core == 1)
+    def _():
+        @pl.loop(0, others)
+        def _(step):
+            pl.semaphore_wait(turn.at[step], 1)
+            far_copy(0, step).start()
 
     q_own.wait()
     for step in range(1, head_count):
         q_copy(step).wait_recv()
 
-    def attend(g, b):
+    pair = 2 if ratio % 2 == 0 else 1
+    scale = HD ** -0.5 * LOG2E
+
+    def query_parts(g, b):
+        q_rows = q_buf[aligned(b, BLK), g * width:(g + 1) * width]
+        for first in range(0, ratio, pair):
+            yield first, jnp.concatenate(
+                [q_rows[:, r * HD:(r + 1) * HD] for r in range(first, first + pair)], axis=0
+            )
+
+    def scores_of(q_part, k_all):
+        return lax.dot_general(
+            q_part, k_all, (((1,), (1,)), ((), ())), preferred_element_type=jnp.float32
+        )
+
+    def near_part(g, b):
         columns = slice(g * HD, (g + 1) * HD)
         near = [ids[b, j] for j in range(NEAR)]
-        far = [ids[b, NEAR + j] for j in range(far_count)]
-        k_all = jnp.concatenate(
-            [k_buf[block, :, columns] for block in near]
-            + [recv_bufs[g][block, :, 0:HD] for block in far], axis=0
-        )
-        v_all = jnp.concatenate(
-            [v_buf[block, :, columns] for block in near]
-            + [recv_bufs[g][block, :, HD:] for block in far], axis=0
-        )
-        q_rows = q_buf[aligned(b, BLK), g * width:(g + 1) * width]
-        pair = 2 if ratio % 2 == 0 else 1
-        for first in range(0, ratio, pair):
-            q_part = jnp.concatenate(
-                [q_rows[:, r * HD:(r + 1) * HD] for r in range(first, first + pair)], axis=0
-            )
-            scores = lax.dot_general(
-                q_part, k_all, (((1,), (1,)), ((), ())), preferred_element_type=jnp.float32
-            )
+        k_all = jnp.concatenate([k_buf[block, :, columns] for block in near], axis=0)
+        v_all = jnp.concatenate([v_buf[block, :, columns] for block in near], axis=0)
+        for first, q_part in query_parts(g, b):
+            scores = scores_of(q_part, k_all)
             highest = jnp.max(scores, axis=1, keepdims=True)
-            exponent = jnp.exp2((scores - highest) * (HD ** -0.5 * LOG2E))
+            exponent = jnp.exp2((scores - highest) * scale)
             total = jnp.sum(exponent, axis=1, keepdims=True)
             mixed = jnp.dot(
+                exponent.astype(jnp.bfloat16), v_all, preferred_element_type=jnp.float32
+            )
+            rows_of = pl.ds(first * BLK, pair * BLK)
+            near_mixed[g, b, rows_of, :] = mixed
+            near_high[g, b, rows_of, :] = jnp.broadcast_to(highest, mixed.shape)
+            near_total[g, b, rows_of, :] = jnp.broadcast_to(total, mixed.shape)
+
+    def far_part(g, b):
+        far = [ids[b, NEAR + j] for j in range(far_count)]
+        k_all = jnp.concatenate([recv_bufs[g][block, :, 0:HD] for block in far], axis=0)
+        v_all = jnp.concatenate([recv_bufs[g][block, :, HD:] for block in far], axis=0)
+        for first, q_part in query_parts(g, b):
+            rows_of = pl.ds(first * BLK, pair * BLK)
+            scores = scores_of(q_part, k_all)
+            before = near_high[g, b, rows_of, :]
+            highest = jnp.maximum(before, jnp.max(scores, axis=1, keepdims=True))
+            factor = jnp.exp2((before - highest) * scale)
+            exponent = jnp.concatenate(
+                [
+                    jnp.exp2((scores[:, j * BLK:(j + 1) * BLK] - highest) * scale)
+                    for j in range(far_count)
+                ],
+                axis=1,
+            )
+            total = near_total[g, b, rows_of, :] * factor + jnp.sum(exponent, axis=1, keepdims=True)
+            mixed = near_mixed[g, b, rows_of, :] * factor + jnp.dot(
                 exponent.astype(jnp.bfloat16), v_all, preferred_element_type=jnp.float32
             )
             result = (mixed / total).astype(jnp.bfloat16)
@@ -178,6 +235,19 @@
                 )
 
     for g in range(kv_local):
+        @pl.loop(0, head_count * per_head)
+        def _(b):
+            near_part(g, b)
+
+    for g in range(kv_local):
+        if g + 1 < kv_local:
+            if g == 0:
+                @pl.when(core == 1)
+                def _():
+                    advance(0)
+            else:
+                advance(g)
+
         @pl.loop(0, others)
         def _(step):
             far_copy(g, step).wait_recv()
@@ -186,12 +256,12 @@
         def _(index):
             step = head_count - 1 - index // per_head
             j = index % per_head
-            attend(g, head_peer(step) * per_head + j)
+            far_part(g, head_peer(step) * per_head + j)
             out_copy(g, step, j).start()
 
         @pl.loop(0, per_head)
         def _(j):
-            attend(g, head * per_head + j)
+            far_part(g, head * per_head + j)
             own_copy(g, j).start()
 
     for step in range(others):
@@ -278,6 +348,10 @@
             dma((kv_local, head_count - 1, per_head)),
             dma((kv_local, per_head)),
             dma((4,)),
+            pltpu.SemaphoreType.REGULAR((others,)),
+            pltpu.VMEM((kv_local, q_count, ratio * BLK, HD), jnp.float32),
+            pltpu.VMEM((kv_local, q_count, ratio * BLK, HD), jnp.float32),
+            pltpu.VMEM((kv_local, q_count, ratio * BLK, HD), jnp.float32),
         ],
         compiler_params=pltpu.CompilerParams(
             collective_id=0, has_side_effects=True, vmem_limit_bytes=56 * 2**20

time: 173 us -> 177 us (1.023)
  the two profiles are of different devices: /device:TPU:10 before, /device:TPU:17 now
where the time goes in v2:
time: 177 us; the launch traced here: 176 us
  Pallas kernels  169 us (95%)
  local copies, waits for them, and re-layouts  5.63 us (3%)
  other arithmetic  1.97 us (1%)
    pallas_call x1, Pallas kernels, shards(): pl.pallas_call(functools.partial(kernel, seq_count, head_count, capacity,...  169 us
    unnamed x3, local copies, waits for them, and re-layouts  4.78 us

profile of v2, /device:TPU:17, one launch (start us, length us, event | category | flops | bytes accessed | tf_op | source)
XLA Modules:
  0.0 176.3 jit_solution(9361970319818691819)
XLA Ops:
  0.0 0.7 slice.7
  0.7 0.1 copy.12
  0.8 0.1 reshape.202
  0.9 0.2 convert_reduce_fusion
  1.1 0.1 iota_compare_fusion.1
  1.2 0.1 iota_compare_fusion
  1.2 0.1 reduce_sum.21
  1.4 0.8 copy.11
  2.1 0.7 pad_add_fusion.ids
  2.8 0.1 broadcast_and_fusion
  2.9 0.8 select_reduce_fusion.asked
  3.7 168.6 %shard_map.46 = bf16[384,4096]{1,0:T(8,128)(2,1)} custom-call(s32[12,8]{1,0:T(8,128)} %pad_add_fusion.ids, s32[7,8,128]{2,1,0:T(8,128)} %select_reduce_fusion.asked, bf16[384,4096]{1,0:T(8,128)(2,1)} %queries.1, bf16[64,128,256]{2,1,0:T(8,128)(2,1)} %bitcast.3, bf16[64,128,256]{2,1,0:T(8,128)(2,1)} %bitcast.4), custom_call_target="tpu_custom_call" | custom-call | tf_op jit(solution)/shard_map/pallas_call | solution.py:324
  172.4 3.9 %copy.14 = bf16[384,4096]{1,0:T(8,128)(2,1)} copy(bf16[384,4096]{1,0:T(8,128)(2,1)} %shard_map.46) | data formatting | bytes 6291456
  (4 shorter events, 0.1 us)

commit v3 on v2

--- a/solution.py
+++ b/solution.py
@@ -11,6 +11,7 @@
 HD = 128
 BLK = 128
 NEAR = 5
+PIECES = 8
 MESH = pl.DeviceIdType.MESH
 LOG2E = math.log2(math.e)
 
@@ -21,9 +22,9 @@
 
 def kernel(
     seq_count, head_count, capacity, kv_local, ratio, per_head, far_count,
-    ids, asked, queries, keys, values, out,
+    ids, slots_of, asked, queries, keys, values, out,
     k_buf, v_buf, q_buf, got, wanted, send_bufs, recv_bufs, stage,
-    id_send, id_recv, q_send, q_recv, f_send, f_recv, o_send, o_recv, o_local, local, turn, near_mixed, near_high, near_total,
+    id_send, id_recv, q_send, q_recv, f_send, f_recv, o_send, o_recv, o_local, local, near_mixed, near_high, near_total,
 ):
     seq = lax.axis_index("seq")
     head = lax.axis_index("head")
@@ -31,6 +32,14 @@
     rows = queries.shape[0]
     q_width = q_buf.shape[1]
     width = ratio * HD
+
+    def seq_peer(step):
+        peer = 0
+        weight = 1
+        while weight < seq_count:
+            peer += (seq // weight + (step + 1) // weight) % 2 * weight
+            weight *= 2
+        return peer
 
     def head_peer(step):
         return (head // 2 + step // 2) % 2 * 2 + (head % 2 + step % 2) % 2
@@ -45,9 +54,9 @@
     q_own.start()
 
     barrier = pltpu.get_barrier_semaphore()
-    for step in range(1, seq_count):
+    for step in range(others):
         pl.semaphore_signal(
-            barrier, inc=1, device_id={"seq": (seq + step) % seq_count}, device_id_type=MESH
+            barrier, inc=1, device_id={"seq": seq_peer(step)}, device_id_type=MESH
         )
     for step in range(1, head_count):
         pl.semaphore_signal(
@@ -61,7 +70,7 @@
             dst_ref=got.at[step],
             send_sem=id_send.at[step],
             recv_sem=id_recv.at[step],
-            device_id={"seq": (seq + seq_count - 1 - step) % seq_count},
+            device_id={"seq": seq_peer(step)},
             device_id_type=MESH,
         )
 
@@ -83,7 +92,7 @@
             dst_ref=recv_bufs[g].at[block],
             send_sem=f_send.at[g, step],
             recv_sem=f_recv.at[g, step],
-            device_id={"seq": (seq + 1 + step) % seq_count},
+            device_id={"seq": seq_peer(step)},
             device_id_type=MESH,
         )
 
@@ -127,18 +136,16 @@
 
     core = head % 2
 
-    @pl.when(core == 0)
-    def _():
-        @pl.loop(0, others)
-        def _(step):
-            gather(0, step)
-            far_copy(0, step).start()
-
-    @pl.when(core == 1)
-    def _():
-        @pl.loop(0, others)
-        def _(step):
-            gather(0, step)
+    def peer_at(index):
+        turned = (index + core) % others
+        odd = turned % 2
+        return (1 - odd) * (seq_count // 2 + turned // 2) + odd * ((turned + 1) // 2) - 1
+
+    @pl.loop(0, others)
+    def _(index):
+        step = peer_at(index)
+        gather(0, step)
+        far_copy(0, step).start()
 
     for g in range(1, kv_local):
         @pl.loop(0, others)
@@ -147,28 +154,13 @@
 
     def advance(g):
         @pl.loop(0, others)
-        def _(step):
+        def _(index):
+            step = peer_at(index)
             far_copy(g, step).wait_send()
-            if g + 1 < kv_local:
-                far_copy(g + 1, step).start()
-
-    @pl.when(core == 0)
-    def _():
-        @pl.loop(0, others)
-        def _(step):
-            far_copy(0, step).wait_send()
-            pl.semaphore_signal(
-                turn.at[step], inc=1, device_id={"head": head_peer(1)}, device_id_type=MESH
-            )
-            if kv_local > 1:
-                far_copy(1, step).start()
-
-    @pl.when(core == 1)
-    def _():
-        @pl.loop(0, others)
-        def _(step):
-            pl.semaphore_wait(turn.at[step], 1)
-            far_copy(0, step).start()
+            far_copy(g + 1, step).start()
+
+    if kv_local > 1:
+        advance(0)
 
     q_own.wait()
     for step in range(1, head_count):
@@ -191,7 +183,7 @@
 
     def near_part(g, b):
         columns = slice(g * HD, (g + 1) * HD)
-        near = [ids[b, j] for j in range(NEAR)]
+        near = [lax.rem(ids[j, b], k_buf.shape[0]) for j in range(NEAR)]
         k_all = jnp.concatenate([k_buf[block, :, columns] for block in near], axis=0)
         v_all = jnp.concatenate([v_buf[block, :, columns] for block in near], axis=0)
         for first, q_part in query_parts(g, b):
@@ -208,7 +200,7 @@
             near_total[g, b, rows_of, :] = jnp.broadcast_to(total, mixed.shape)
 
     def far_part(g, b):
-        far = [ids[b, NEAR + j] for j in range(far_count)]
+        far = [slots_of[j, b] for j in range(far_count)]
         k_all = jnp.concatenate([recv_bufs[g][block, :, 0:HD] for block in far], axis=0)
         v_all = jnp.concatenate([recv_bufs[g][block, :, HD:] for block in far], axis=0)
         for first, q_part in query_parts(g, b):
@@ -240,13 +232,8 @@
             near_part(g, b)
 
     for g in range(kv_local):
-        if g + 1 < kv_local:
-            if g == 0:
-                @pl.when(core == 1)
-                def _():
-                    advance(0)
-            else:
-                advance(g)
+        if 0 < g < kv_local - 1:
+            advance(g)
 
         @pl.loop(0, others)
         def _(step):
@@ -279,6 +266,20 @@
         @pl.loop(0, per_head)
         def _(j):
             own_copy(g, j).wait()
+
+
+def hand_over(landed, out, done):
+    size = out.shape[0] // PIECES
+    copies = [
+        pltpu.make_async_copy(
+            landed.at[pl.ds(piece * size, size)], out.at[pl.ds(piece * size, size)], done.at[piece]
+        )
+        for piece in range(PIECES)
+    ]
+    for copy in copies:
+        copy.start()
+    for copy in copies:
+        copy.wait()
 
 
 def shards(queries, cache_keys, cache_values, block_ids):
@@ -296,16 +297,16 @@
     others = seq_count - 1
     capacity = max(2, (far_count * q_count + seq_count - 2) // others)
 
-    near = block_ids[:, :NEAR] - seq * k_count
-    far = block_ids[:, NEAR:].reshape(-1)
+    ids = block_ids.T
+    far = ids[NEAR:].reshape(-1)
     owner = far // k_count
     within = far - owner * k_count
-    distance = (seq - owner + seq_count) % seq_count - 1
+    distance = (seq ^ owner) - 1
     order = jnp.arange(far.shape[0], dtype=jnp.int32)
     earlier = (distance[:, None] == distance[None, :]) & (order[None, :] < order[:, None])
     rank = jnp.sum(earlier.astype(jnp.int32), axis=1)
     slot = distance * capacity + rank
-    ids = jnp.concatenate([near, slot.reshape(q_count, far_count)], axis=1)
+    slots_of = slot.reshape(far_count, q_count)
     lane = jnp.arange(128, dtype=jnp.int32)[None, None, None, :]
     shape = (far.shape[0], others, 8, 128)
     hit = (
@@ -321,12 +322,13 @@
     bf16 = jnp.bfloat16
     dma = pltpu.SemaphoreType.DMA
     anywhere = pl.BlockSpec(memory_space=pl.ANY)
-    return pl.pallas_call(
+    landed = pl.pallas_call(
         functools.partial(
             kernel, seq_count, head_count, capacity, kv_local, ratio, per_head, far_count
         ),
         out_shape=jax.ShapeDtypeStruct((rows, q_columns), bf16),
         in_specs=[
+            pl.BlockSpec(memory_space=pltpu.SMEM),
             pl.BlockSpec(memory_space=pltpu.SMEM),
             pl.BlockSpec(memory_space=pltpu.VMEM),
             anywhere, anywhere, anywhere,
@@ -348,7 +350,6 @@
             dma((kv_local, head_count - 1, per_head)),
             dma((kv_local, per_head)),
             dma((4,)),
-            pltpu.SemaphoreType.REGULAR((others,)),
             pltpu.VMEM((kv_local, q_count, ratio * BLK, HD), jnp.float32),
             pltpu.VMEM((kv_local, q_count, ratio * BLK, HD), jnp.float32),
             pltpu.VMEM((kv_local, q_count, ratio * BLK, HD), jnp.float32),
@@ -356,7 +357,15 @@
         compiler_params=pltpu.CompilerParams(
             collective_id=0, has_side_effects=True, vmem_limit_bytes=56 * 2**20
         ),
-    )(ids, asked, queries, cache_keys.reshape(blocks), cache_values.reshape(blocks))
+    )(ids, slots_of, asked, queries, cache_keys.reshape(blocks), cache_values.reshape(blocks))
+    return pl.pallas_call(
+        hand_over,
+        out_shape=jax.ShapeDtypeStruct((rows, q_columns), bf16),
+        in_specs=[anywhere],
+        out_specs=anywhere,
+        scratch_shapes=[dma((PIECES,))],
+        compiler_params=pltpu.CompilerParams(vmem_limit_bytes=62 * 2**20),
+    )(landed)
 
 
 def solution(mesh):

time: 177 us -> 263 us (1.49)
  the two profiles are of different devices: /device:TPU:17 before, /device:TPU:10 now
where the time goes in v3:
time: 263 us
  Pallas kernels  260 us (99%)
    pallas_call x1, Pallas kernels, shards(): pl.pallas_call(functools.partial(kernel, seq_count, head_count, capacity,...  163 us
    pallas_call x1, Pallas kernels, shards(): pl.pallas_call(hand_over, out_shape=jax.ShapeDtypeStruct((rows, q_columns...  96.5 us

profile of v3, /device:TPU:10, one launch (start us, length us, event | category | flops | bytes accessed | tf_op | source)
XLA Modules:
  0.0 263.0 jit_solution(13713736410713178964)
XLA Ops:
  0.0 0.7 slice.3
  0.7 0.1 reshape.166
  0.8 0.2 convert_reduce_fusion
  1.0 0.1 reduce_sum.21
  1.1 1.3 fusion.5.slots_of
  2.4 0.1 iota_compare_fusion
  2.4 0.1 iota_compare_fusion.1
  2.5 0.1 broadcast_and_fusion
  2.6 0.8 select_reduce_fusion.asked
  3.4 163.1 %shard_map.46.landed = bf16[384,4096]{1,0:T(8,128)(2,1)} custom-call(s32[8,12]{1,0:T(8,128)} %bitcast.7, s32[3,12]{1,0:T(4,128)} %fusion.5.slots_of, s32[7,8,128]{2,1,0:T(8,128)} %select_reduce_fusion.asked, bf16[384,4096]{1,0:T(8,128)(2,1)} %queries.1, bf16[64,128,256]{2,1,0:T(8,128)(2,1)} %bitcast.3, bf16[64,128,256]{2,1,0:T(8,128)(2,1)} %bitcast.4), custom_call_target="tpu_custom_call" | custom-call | tf_op jit(solution)/shard_map/pallas_call | solution.py:325
  166.5 96.5 %shard_map.47 = bf16[384,4096]{1,0:T(8,128)(2,1)} custom-call(bf16[384,4096]{1,0:T(8,128)(2,1)} %shard_map.46.landed), custom_call_target="tpu_custom_call" | custom-call | tf_op jit(solution)/shard_map/pallas_call | solution.py:361
  (2 shorter events, 0.0 us)

commit v4 on v3

--- a/solution.py
+++ b/solution.py
@@ -11,7 +11,7 @@
 HD = 128
 BLK = 128
 NEAR = 5
-PIECES = 8
+TILE = 64
 MESH = pl.DeviceIdType.MESH
 LOG2E = math.log2(math.e)
 
@@ -22,16 +22,22 @@
 
 def kernel(
     seq_count, head_count, capacity, kv_local, ratio, per_head, far_count,
-    ids, slots_of, asked, queries, keys, values, out,
-    k_buf, v_buf, q_buf, got, wanted, send_bufs, recv_bufs, stage,
-    id_send, id_recv, q_send, q_recv, f_send, f_recv, o_send, o_recv, o_local, local, near_mixed, near_high, near_total,
+    ids, slots_of, asked, queries, keys, values, *rest
 ):
+    landed, rest = rest[:kv_local + 1], rest[kv_local + 1:]
+    (
+        k_buf, v_buf, q_buf, got, wanted, send_bufs, recv_bufs, stages,
+        id_send, id_recv, q_send, q_recv, f_send, f_recv, o_send, o_recv, o_local, local,
+        near_mixed, near_high, near_total, far_weight,
+    ) = rest
     seq = lax.axis_index("seq")
     head = lax.axis_index("head")
     others = seq_count - 1
     rows = queries.shape[0]
     q_width = q_buf.shape[1]
     width = ratio * HD
+    last = kv_local - 1
+    half = HD // 2
 
     def seq_peer(step):
         peer = 0
@@ -96,22 +102,24 @@
             device_id_type=MESH,
         )
 
-    def out_copy(g, step, j):
+    def place(part, j):
+        span = stages[part].shape[2]
+        return landed[part].at[aligned(j, BLK), aligned(head, span)]
+
+    def out_copy(part, step, j):
         peer = head_peer(step)
         return pltpu.make_async_remote_copy(
-            src_ref=stage.at[g, peer * per_head + j],
-            dst_ref=out.at[aligned(j, BLK), pl.ds(pl.multiple_of(head * q_width + g * width, width), width)],
-            send_sem=o_send.at[g, step - 1, j],
-            recv_sem=o_recv.at[g, step - 1, j],
+            src_ref=stages[part].at[peer * per_head + j],
+            dst_ref=place(part, j),
+            send_sem=o_send.at[part, step - 1, j],
+            recv_sem=o_recv.at[part, step - 1, j],
             device_id={"head": peer},
             device_id_type=MESH,
         )
 
-    def own_copy(g, j):
+    def own_copy(part, j):
         return pltpu.make_async_copy(
-            stage.at[g, head * per_head + j],
-            out.at[aligned(j, BLK), pl.ds(pl.multiple_of(head * q_width + g * width, width), width)],
-            o_local.at[g, j],
+            stages[part].at[head * per_head + j], place(part, j), o_local.at[part, j]
         )
 
     for step in range(others):
@@ -130,9 +138,18 @@
         columns = slice(g * HD, (g + 1) * HD)
         for slot in range(capacity):
             block = wanted[step, 0, slot]
-            place = step * capacity + slot
-            send_bufs[g][place, :, 0:HD] = k_buf[block, :, columns]
-            send_bufs[g][place, :, HD:] = v_buf[block, :, columns]
+            spot = step * capacity + slot
+            if g < last:
+                send_bufs[g][spot, :, 0:HD] = k_buf[block, :, columns]
+                send_bufs[g][spot, :, HD:] = v_buf[block, :, columns]
+            else:
+                send_bufs[g][spot] = k_buf[block, :, columns]
+                value = v_buf[block, :, columns]
+                for part in range(2):
+                    side = value[:, part * half:(part + 1) * half]
+                    send_bufs[g + 1 + part][spot] = jnp.concatenate(
+                        [side[:BLK // 2], side[BLK // 2:]], axis=1
+                    )
 
     core = head % 2
 
@@ -158,9 +175,6 @@
             step = peer_at(index)
             far_copy(g, step).wait_send()
             far_copy(g + 1, step).start()
-
-    if kv_local > 1:
-        advance(0)
 
     q_own.wait()
     for step in range(1, head_count):
@@ -195,9 +209,9 @@
                 exponent.astype(jnp.bfloat16), v_all, preferred_element_type=jnp.float32
             )
             rows_of = pl.ds(first * BLK, pair * BLK)
-            near_mixed[g, b, rows_of, :] = mixed
-            near_high[g, b, rows_of, :] = jnp.broadcast_to(highest, mixed.shape)
-            near_total[g, b, rows_of, :] = jnp.broadcast_to(total, mixed.shape)
+            near_mixed[b, rows_of, :] = mixed
+            near_high[b, rows_of, :] = jnp.broadcast_to(highest, mixed.shape)
+            near_total[b, rows_of, :] = jnp.broadcast_to(total, mixed.shape)
 
     def far_part(g, b):
         far = [slots_of[j, b] for j in range(far_count)]
@@ -206,7 +220,7 @@
         for first, q_part in query_parts(g, b):
             rows_of = pl.ds(first * BLK, pair * BLK)
             scores = scores_of(q_part, k_all)
-            before = near_high[g, b, rows_of, :]
+            before = near_high[b, rows_of, :]
             highest = jnp.maximum(before, jnp.max(scores, axis=1, keepdims=True))
             factor = jnp.exp2((before - highest) * scale)
             exponent = jnp.concatenate(
@@ -216,70 +230,125 @@
                 ],
                 axis=1,
             )
-            total = near_total[g, b, rows_of, :] * factor + jnp.sum(exponent, axis=1, keepdims=True)
-            mixed = near_mixed[g, b, rows_of, :] * factor + jnp.dot(
+            total = near_total[b, rows_of, :] * factor + jnp.sum(exponent, axis=1, keepdims=True)
+            mixed = near_mixed[b, rows_of, :] * factor + jnp.dot(
                 exponent.astype(jnp.bfloat16), v_all, preferred_element_type=jnp.float32
             )
             result = (mixed / total).astype(jnp.bfloat16)
             for r in range(pair):
-                stage[g, b, :, (first + r) * HD:(first + r + 1) * HD] = (
+                stages[g][b, :, (first + r) * HD:(first + r + 1) * HD] = (
                     result[r * BLK:(r + 1) * BLK]
                 )
+
+    def weigh_part(b):
+        far = [slots_of[j, b] for j in range(far_count)]
+        k_all = jnp.concatenate([recv_bufs[last][block] for block in far], axis=0)
+        for first, q_part in query_parts(last, b):
+            rows_of = pl.ds(first * BLK, pair * BLK)
+            scores = scores_of(q_part, k_all)
+            before = near_high[b, rows_of, :]
+            highest = jnp.maximum(before, jnp.max(scores, axis=1, keepdims=True))
+            factor = jnp.exp2((before - highest) * scale)
+            exponent = jnp.concatenate(
+                [
+                    jnp.exp2((scores[:, j * BLK:(j + 1) * BLK] - highest) * scale)
+                    for j in range(far_count)
+                ],
+                axis=1,
+            )
+            total = near_total[b, rows_of, :] * factor + jnp.sum(exponent, axis=1, keepdims=True)
+            near_total[b, rows_of, :] = 1.0 / total
+            near_mixed[b, rows_of, :] = near_mixed[b, rows_of, :] * factor
+            far_weight[b, rows_of, :] = exponent.astype(jnp.bfloat16)
+
+    def blend_part(part, b):
+        far = [slots_of[j, b] for j in range(far_count)]
+        sides = []
+        for block in far:
+            packed = recv_bufs[last + 1 + part][block]
+            sides += [packed[:, :half], packed[:, half:]]
+        v_all = jnp.concatenate(sides, axis=0)
+        pieces = []
+        for first in range(0, ratio, pair):
+            rows_of = pl.ds(first * BLK, pair * BLK)
+            mixed = near_mixed[b, rows_of, part * half:(part + 1) * half] + jnp.dot(
+                far_weight[b, rows_of, :], v_all, preferred_element_type=jnp.float32
+            )
+            result = (mixed * near_total[b, rows_of, 0:half]).astype(jnp.bfloat16)
+            pieces += [result[r * BLK:(r + 1) * BLK] for r in range(pair)]
+        stages[last + part][b] = jnp.concatenate(pieces, axis=1)
+
+    def arrive(piece):
+        @pl.loop(0, others)
+        def _(step):
+            far_copy(piece, step).wait_recv()
+
+    def hand_out(part, finish):
+        @pl.loop(0, (head_count - 1) * per_head)
+        def _(index):
+            step = head_count - 1 - index // per_head
+            j = index % per_head
+            finish(head_peer(step) * per_head + j)
+            out_copy(part, step, j).start()
+
+        @pl.loop(0, per_head)
+        def _(j):
+            finish(head * per_head + j)
+            own_copy(part, j).start()
 
     for g in range(kv_local):
         @pl.loop(0, head_count * per_head)
         def _(b):
             near_part(g, b)
 
-    for g in range(kv_local):
-        if 0 < g < kv_local - 1:
-            advance(g)
-
-        @pl.loop(0, others)
-        def _(step):
-            far_copy(g, step).wait_recv()
-
+        advance(g)
+        arrive(g)
+        if g < last:
+            hand_out(g, functools.partial(far_part, g))
+
+    @pl.loop(0, head_count * per_head)
+    def _(b):
+        weigh_part(b)
+
+    advance(last + 1)
+    arrive(last + 1)
+    hand_out(last, functools.partial(blend_part, 0))
+    arrive(last + 2)
+    hand_out(last + 1, functools.partial(blend_part, 1))
+
+    for step in range(others):
+        id_copy(step).wait_send()
+        far_copy(last + 2, step).wait_send()
+    for step in range(1, head_count):
+        q_copy(step).wait_send()
+    for part in range(kv_local + 1):
         @pl.loop(0, (head_count - 1) * per_head)
         def _(index):
             step = head_count - 1 - index // per_head
             j = index % per_head
-            far_part(g, head_peer(step) * per_head + j)
-            out_copy(g, step, j).start()
+            out_copy(part, step, j).wait()
 
         @pl.loop(0, per_head)
         def _(j):
-            far_part(g, head * per_head + j)
-            own_copy(g, j).start()
-
-    for step in range(others):
-        id_copy(step).wait_send()
-        far_copy(kv_local - 1, step).wait_send()
-    for step in range(1, head_count):
-        q_copy(step).wait_send()
-    for g in range(kv_local):
-        @pl.loop(0, (head_count - 1) * per_head)
-        def _(index):
-            step = head_count - 1 - index // per_head
-            j = index % per_head
-            out_copy(g, step, j).wait()
-
-        @pl.loop(0, per_head)
-        def _(j):
-            own_copy(g, j).wait()
-
-
-def hand_over(landed, out, done):
-    size = out.shape[0] // PIECES
-    copies = [
-        pltpu.make_async_copy(
-            landed.at[pl.ds(piece * size, size)], out.at[pl.ds(piece * size, size)], done.at[piece]
-        )
-        for piece in range(PIECES)
-    ]
-    for copy in copies:
-        copy.start()
-    for copy in copies:
-        copy.wait()
+            own_copy(part, j).wait()
+
+
+def side_by_side(head_count, ratio, whole_count, *refs):
+    *wholes, left, right, out = refs
+    half = HD // 2
+    width = ratio * HD
+    for head in range(head_count):
+        start = head * (whole_count + 1) * width
+        for g in range(whole_count):
+            out[:, start + g * width:start + (g + 1) * width] = (
+                wholes[g][:, head * width:(head + 1) * width]
+            )
+        start += whole_count * width
+        for r in range(ratio):
+            column = (head * ratio + r) * half
+            out[:, start + r * HD:start + (r + 1) * HD] = jnp.concatenate(
+                [left[:, column:column + half], right[:, column:column + half]], axis=1
+            )
 
 
 def shards(queries, cache_keys, cache_values, block_ids):
@@ -320,52 +389,57 @@
     slots = others * capacity
     blocks = (k_count, BLK, cache_keys.shape[1])
     bf16 = jnp.bfloat16
+    width = ratio * HD
+    spans = [width] * (kv_local - 1) + [width // 2] * 2
+    pieces = [(slots, BLK, 2 * HD)] * (kv_local - 1)
+    pieces += [(slots, BLK, HD)] + [(slots, BLK // 2, HD)] * 2
     dma = pltpu.SemaphoreType.DMA
     anywhere = pl.BlockSpec(memory_space=pl.ANY)
     landed = pl.pallas_call(
         functools.partial(
             kernel, seq_count, head_count, capacity, kv_local, ratio, per_head, far_count
         ),
-        out_shape=jax.ShapeDtypeStruct((rows, q_columns), bf16),
+        out_shape=[jax.ShapeDtypeStruct((rows, head_count * span), bf16) for span in spans],
         in_specs=[
             pl.BlockSpec(memory_space=pltpu.SMEM),
             pl.BlockSpec(memory_space=pltpu.SMEM),
             pl.BlockSpec(memory_space=pltpu.VMEM),
             anywhere, anywhere, anywhere,
         ],
-        out_specs=anywhere,
+        out_specs=[anywhere for _ in spans],
         scratch_shapes=[
             pltpu.VMEM(blocks, bf16),
             pltpu.VMEM(blocks, bf16),
             pltpu.VMEM((rows * head_count, q_width), bf16),
             pltpu.VMEM((others, 8, 128), jnp.int32),
             pltpu.SMEM((others, 8, 128), jnp.int32),
-            [pltpu.VMEM((slots, BLK, 2 * HD), bf16) for _ in range(kv_local)],
-            [pltpu.VMEM((slots, BLK, 2 * HD), bf16) for _ in range(kv_local)],
-            pltpu.VMEM((kv_local, q_count, BLK, ratio * HD), bf16),
+            [pltpu.VMEM(piece, bf16) for piece in pieces],
+            [pltpu.VMEM(piece, bf16) for piece in pieces],
+            [pltpu.VMEM((q_count, BLK, span), bf16) for span in spans],
             dma((others,)), dma((others,)),
             dma((head_count - 1,)), dma((head_count - 1,)),
-            dma((kv_local, others)), dma((kv_local, others)),
-            dma((kv_local, head_count - 1, per_head)),
-            dma((kv_local, head_count - 1, per_head)),
-            dma((kv_local, per_head)),
+            dma((len(pieces), others)), dma((len(pieces), others)),
+            dma((len(spans), head_count - 1, per_head)),
+            dma((len(spans), head_count - 1, per_head)),
+            dma((len(spans), per_head)),
             dma((4,)),
-            pltpu.VMEM((kv_local, q_count, ratio * BLK, HD), jnp.float32),
-            pltpu.VMEM((kv_local, q_count, ratio * BLK, HD), jnp.float32),
-            pltpu.VMEM((kv_local, q_count, ratio * BLK, HD), jnp.float32),
+            pltpu.VMEM((q_count, ratio * BLK, HD), jnp.float32),
+            pltpu.VMEM((q_count, ratio * BLK, HD), jnp.float32),
+            pltpu.VMEM((q_count, ratio * BLK, HD), jnp.float32),
+            pltpu.VMEM((q_count, ratio * BLK, far_count * BLK), bf16),
         ],
         compiler_params=pltpu.CompilerParams(
             collective_id=0, has_side_effects=True, vmem_limit_bytes=56 * 2**20
         ),
     )(ids, slots_of, asked, queries, cache_keys.reshape(blocks), cache_values.reshape(blocks))
     return pl.pallas_call(
-        hand_over,
+        functools.partial(side_by_side, head_count, ratio, kv_local - 1),
+        grid=(rows // TILE,),
         out_shape=jax.ShapeDtypeStruct((rows, q_columns), bf16),
-        in_specs=[anywhere],
-        out_specs=anywhere,
-        scratch_shapes=[dma((PIECES,))],
+        in_specs=[pl.BlockSpec((TILE, head_count * span), lambda i: (i, 0)) for span in spans],
+        out_specs=pl.BlockSpec((TILE, q_columns), lambda i: (i, 0)),
         compiler_params=pltpu.CompilerParams(vmem_limit_bytes=62 * 2**20),
-    )(landed)
+    )(*landed)
 
 
 def solution(mesh):

time: 263 us -> 170 us (0.65); the launches traced: 263 us -> 166 us
  Pallas kernels: 260 us -> 163 us
    pallas_call x1, Pallas kernels: 96.5 us -> 5.57 us  [shards(): pl.pallas_call(functools.partial(side_by_side, head_count, ratio, kv_loca...]
    pallas_call x1, Pallas kernels: 163 us -> 157 us  [shards(): pl.pallas_call(functools.partial(kernel, seq_count, head_count, capacity,...]
where the time goes in v4:
time: 170 us; the launch traced here: 166 us
  Pallas kernels  163 us (96%)
  other arithmetic  2.54 us (1%)
    pallas_call x1, Pallas kernels, shards(): pl.pallas_call(functools.partial(kernel, seq_count, head_count, capacity,...  157 us
    pallas_call x1, Pallas kernels, shards(): pl.pallas_call(functools.partial(side_by_side, head_count, ratio, kv_loca...  5.57 us

profile of v4, /device:TPU:10, one launch (start us, length us, event | category | flops | bytes accessed | tf_op | source)
XLA Modules:
  0.0 166.4 jit_solution(209036829503022651)
XLA Ops:
  0.0 0.7 slice.3
  0.7 0.1 reshape.166
  0.8 0.2 convert_reduce_fusion
  1.0 0.1 reduce_sum.21
  1.1 1.3 fusion.5.slots_of
  2.4 0.1 iota_compare_fusion
  2.4 0.1 iota_compare_fusion.1
  2.5 0.1 broadcast_and_fusion
  2.6 0.8 select_reduce_fusion.asked
  3.4 157.4 %shard_map.46 = (bf16[384,2048]{1,0:T(8,128)(2,1)}, bf16[384,1024]{1,0:T(8,128)(2,1)}, bf16[384,1024]{1,0:T(8,128)(2,1)}) custom-call(s32[8,12]{1,0:T(8,128)} %bitcast.7, s32[3,12]{1,0:T(4,128)} %fusion.5.slots_of, s32[7,8,128]{2,1,0:T(8,128)} %select_reduce_fusion.asked, bf16[384,4096]{1,0:T(8,128)(2,1)} %queries.1, bf16[64,128,256]{2,1,0:T(8,128)(2,1)} %bitcast.3, ...), custom_call_target="tpu_custom_call" | custom-call | tf_op jit(solution)/shard_map/pallas_call | solution.py:398
  160.9 5.6 %shard_map.47 = bf16[384,4096]{1,0:T(8,128)(2,1)} custom-call(bf16[384,2048]{1,0:T(8,128)(2,1)} %get-tuple-element.8.refs_0_, bf16[384,1024]{1,0:T(8,128)(2,1)} %get-tuple-element.9.refs_1_, bf16[384,1024]{1,0:T(8,128)(2,1)} %get-tuple-element.10.refs_2_), custom_call_target="tpu_custom_call" | custom-call | tf_op jit(solution)/shard_map/pallas_call | solution.py:435
  (2 shorter events, 0.0 us)

commit v5 on v4

--- a/solution.py
+++ b/solution.py
@@ -12,6 +12,7 @@
 BLK = 128
 NEAR = 5
 TILE = 64
+CHUNKS = 2
 MESH = pl.DeviceIdType.MESH
 LOG2E = math.log2(math.e)
 
@@ -91,13 +92,15 @@
             device_id_type=MESH,
         )
 
-    def far_copy(g, step):
-        block = pl.ds(step * capacity, capacity)
+    chunk = capacity // CHUNKS
+
+    def far_copy(g, part, step):
+        block = pl.ds(step * capacity + part * chunk, chunk)
         return pltpu.make_async_remote_copy(
             src_ref=send_bufs[g].at[block],
             dst_ref=recv_bufs[g].at[block],
-            send_sem=f_send.at[g, step],
-            recv_sem=f_recv.at[g, step],
+            send_sem=f_send.at[g, part, step],
+            recv_sem=f_recv.at[g, part, step],
             device_id={"seq": seq_peer(step)},
             device_id_type=MESH,
         )
@@ -162,19 +165,24 @@
     def _(index):
         step = peer_at(index)
         gather(0, step)
-        far_copy(0, step).start()
+        far_copy(0, 0, step).start()
+
+    for part in range(1, CHUNKS):
+        @pl.loop(0, others)
+        def _(index):
+            far_copy(0, part, peer_at(index)).start()
 
     for g in range(1, kv_local):
         @pl.loop(0, others)
         def _(step):
             gather(g, step)
 
-    def advance(g):
+    def advance(g, part):
         @pl.loop(0, others)
         def _(index):
             step = peer_at(index)
-            far_copy(g, step).wait_send()
-            far_copy(g + 1, step).start()
+            far_copy(g, part, step).wait_send()
+            far_copy(g + 1, part, step).start()
 
     q_own.wait()
     for step in range(1, head_count):
@@ -281,7 +289,8 @@
     def arrive(piece):
         @pl.loop(0, others)
         def _(step):
-            far_copy(piece, step).wait_recv()
+            for part in range(CHUNKS):
+                far_copy(piece, part, step).wait_recv()
 
     def hand_out(part, finish):
         @pl.loop(0, (head_count - 1) * per_head)
@@ -297,11 +306,18 @@
             own_copy(part, j).start()
 
     for g in range(kv_local):
+        for part in range(CHUNKS - 1):
+            if g == 0:
+                advance(g, part)
+
         @pl.loop(0, head_count * per_head)
         def _(b):
             near_part(g, b)
 
-        advance(g)
+        for part in range(CHUNKS - 1):
+            if g > 0:
+                advance(g, part)
+        advance(g, CHUNKS - 1)
         arrive(g)
         if g < last:
             hand_out(g, functools.partial(far_part, g))
@@ -310,7 +326,8 @@
     def _(b):
         weigh_part(b)
 
-    advance(last + 1)
+    for part in range(CHUNKS):
+        advance(last + 1, part)
     arrive(last + 1)
     hand_out(last, functools.partial(blend_part, 0))
     arrive(last + 2)
@@ -318,7 +335,8 @@
 
     for step in range(others):
         id_copy(step).wait_send()
-        far_copy(last + 2, step).wait_send()
+        for part in range(CHUNKS):
+            far_copy(last + 2, part, step).wait_send()
     for step in range(1, head_count):
         q_copy(step).wait_send()
     for part in range(kv_local + 1):
@@ -365,6 +383,7 @@
     far_count = picks - NEAR
     others = seq_count - 1
     capacity = max(2, (far_count * q_count + seq_count - 2) // others)
+    capacity += -capacity % CHUNKS
 
     ids = block_ids.T
     far = ids[NEAR:].reshape(-1)
@@ -418,7 +437,7 @@
             [pltpu.VMEM((q_count, BLK, span), bf16) for span in spans],
             dma((others,)), dma((others,)),
             dma((head_count - 1,)), dma((head_count - 1,)),
-            dma((len(pieces), others)), dma((len(pieces), others)),
+            dma((len(pieces), CHUNKS, others)), dma((len(pieces), CHUNKS, others)),
             dma((len(spans), head_count - 1, per_head)),
             dma((len(spans), head_count - 1, per_head)),
             dma((len(spans), per_head)),
@@ -429,7 +448,7 @@
             pltpu.VMEM((q_count, ratio * BLK, far_count * BLK), bf16),
         ],
         compiler_params=pltpu.CompilerParams(
-            collective_id=0, has_side_effects=True, vmem_limit_bytes=56 * 2**20
+            collective_id=0, has_side_effects=True, vmem_limit_bytes=50 * 2**20
         ),
     )(ids, slots_of, asked, queries, cache_keys.reshape(blocks), cache_values.reshape(blocks))
     return pl.pallas_call(
@@ -438,7 +457,6 @@
         out_shape=jax.ShapeDtypeStruct((rows, q_columns), bf16),
         in_specs=[pl.BlockSpec((TILE, head_count * span), lambda i: (i, 0)) for span in spans],
         out_specs=pl.BlockSpec((TILE, q_columns), lambda i: (i, 0)),
-        compiler_params=pltpu.CompilerParams(vmem_limit_bytes=62 * 2**20),
     )(*landed)
 
 

time: 170 us -> 171 us (level)
  local copies, waits for them, and re-layouts: 0.86 us -> 4.49 us
    unnamed x0 -> x8, local copies, waits for them, and re-layouts: none -> 3.63 us
where the time goes in v5:
time: 171 us; the launch traced here: 168 us
  Pallas kernels  162 us (95%)
  local copies, waits for them, and re-layouts  4.49 us (3%)
    pallas_call x1, Pallas kernels, shards(): pl.pallas_call(functools.partial(kernel, seq_count, head_count, capacity,...  156 us
    pallas_call x1, Pallas kernels, shards(): pl.pallas_call(functools.partial(side_by_side, head_count, ratio, kv_loca...  5.55 us
    unnamed x8, local copies, waits for them, and re-layouts  3.63 us

profile of v5, /device:TPU:10, one launch (start us, length us, event | category | flops | bytes accessed | tf_op | source)
XLA Modules:
  0.0 167.7 jit_solution(8879437782513844736)
XLA Ops:
  0.0 0.7 slice.3
  0.7 0.1 reshape.166
  0.8 0.2 convert_reduce_fusion
  1.0 0.1 reduce_sum.21
  1.1 0.7 fusion.5.slots_of
  1.8 0.1 iota_compare_fusion
  1.9 0.1 iota_compare_fusion.1
  1.9 0.1 broadcast_and_fusion
  2.0 0.2 select_reduce_fusion.asked
  2.2 0.0 copy-start.3
  2.2 0.7 copy-done.3
  2.9 156.2 %shard_map.46 = (bf16[384,2048]{1,0:T(8,128)(2,1)S(1)}, bf16[384,1024]{1,0:T(8,128)(2,1)S(1)}, bf16[384,1024]{1,0:T(8,128)(2,1)S(1)}) custom-call(s32[8,12]{1,0:T(8,128)S(1)} %bitcast.5, s32[3,12]{1,0:T(4,128)S(1)} %fusion.5.slots_of, s32[7,8,128]{2,1,0:T(8,128)S(1)} %select_reduce_fusion.asked, bf16[384,4096]{1,0:T(8,128)(2,1)} %queries.1, ...), custom_call_target="tpu_custom_call" | custom-call | tf_op jit(solution)/shard_map/pallas_call | solution.py:417
  159.2 0.0 copy-start
  159.2 1.1 copy-done
  160.3 0.0 copy-start.1
  160.3 0.9 copy-done.1
  161.2 0.0 copy-start.2
  161.2 0.9 copy-done.2
  162.1 5.6 %shard_map.47 = bf16[384,4096]{1,0:T(8,128)(2,1)} custom-call(bf16[384,2048]{1,0:T(8,128)(2,1)} %copy-done, bf16[384,1024]{1,0:T(8,128)(2,1)} %copy-done.1, bf16[384,1024]{1,0:T(8,128)(2,1)} %copy-done.2), custom_call_target="tpu_custom_call" | custom-call | tf_op jit(solution)/shard_map/pallas_call | solution.py:454
  (2 shorter events, 0.0 us)
Async XLA Ops:
  2.2 0.7 copy-start.3
  159.2 1.2 copy-start
  160.3 0.9 copy-start.1
  161.2 0.9 copy-start.2

commit v6 on v5

--- a/solution.py
+++ b/solution.py
@@ -283,7 +283,8 @@
                 far_weight[b, rows_of, :], v_all, preferred_element_type=jnp.float32
             )
             result = (mixed * near_total[b, rows_of, 0:half]).astype(jnp.bfloat16)
-            pieces += [result[r * BLK:(r + 1) * BLK] for r in range(pair)]
+            own = [result[r * BLK:(r + 1) * BLK] for r in range(pair)]
+            pieces += own if part == 0 else own[::-1]
         stages[last + part][b] = jnp.concatenate(pieces, axis=1)
 
     def arrive(piece):
@@ -362,11 +363,15 @@
                 wholes[g][:, head * width:(head + 1) * width]
             )
         start += whole_count * width
-        for r in range(ratio):
+        for r in range(0, ratio, 2):
             column = (head * ratio + r) * half
-            out[:, start + r * HD:start + (r + 1) * HD] = jnp.concatenate(
-                [left[:, column:column + half], right[:, column:column + half]], axis=1
-            )
+            first = left[:, column:column + HD].astype(jnp.float32)
+            second = right[:, column:column + HD].astype(jnp.float32)
+            low = lax.broadcasted_iota(jnp.int32, first.shape, 1) < half
+            even = jnp.where(low, first, second)
+            odd = pltpu.roll(jnp.where(low, second, first), half, 1)
+            out[:, start + r * HD:start + (r + 1) * HD] = even.astype(out.dtype)
+            out[:, start + (r + 1) * HD:start + (r + 2) * HD] = odd.astype(out.dtype)
 
 
 def shards(queries, cache_keys, cache_values, block_ids):
@@ -448,7 +453,7 @@
             pltpu.VMEM((q_count, ratio * BLK, far_count * BLK), bf16),
         ],
         compiler_params=pltpu.CompilerParams(
-            collective_id=0, has_side_effects=True, vmem_limit_bytes=50 * 2**20
+            collective_id=0, has_side_effects=True, vmem_limit_bytes=56 * 2**20
         ),
     )(ids, slots_of, asked, queries, cache_keys.reshape(blocks), cache_values.reshape(blocks))
     return pl.pallas_call(
@@ -457,6 +462,7 @@
         out_shape=jax.ShapeDtypeStruct((rows, q_columns), bf16),
         in_specs=[pl.BlockSpec((TILE, head_count * span), lambda i: (i, 0)) for span in spans],
         out_specs=pl.BlockSpec((TILE, q_columns), lambda i: (i, 0)),
+        compiler_params=pltpu.CompilerParams(vmem_limit_bytes=62 * 2**20),
     )(*landed)
 
 

time: 171 us -> 169 us (0.988)
  local copies, waits for them, and re-layouts: 4.49 us -> 0.86 us
    unnamed x8 -> x0, local copies, waits for them, and re-layouts: 3.63 us -> none
where the time goes in v6:
time: 169 us; the launch traced here: 165 us
  Pallas kernels  162 us (96%)
  other arithmetic  2.54 us (2%)
    pallas_call x1, Pallas kernels, shards(): pl.pallas_call(functools.partial(kernel, seq_count, head_count, capacity,...  156 us
    pallas_call x1, Pallas kernels, shards(): pl.pallas_call(functools.partial(side_by_side, head_count, ratio, kv_loca...  5.51 us

profile of v6, /device:TPU:10, one launch (start us, length us, event | category | flops | bytes accessed | tf_op | source)
XLA Modules:
  0.0 165.4 jit_solution(4300194106782028719)
XLA Ops:
  0.0 0.7 slice.3
  0.7 0.1 reshape.166
  0.8 0.2 convert_reduce_fusion
  1.0 0.1 reduce_sum.21
  1.1 1.3 fusion.5.slots_of
  2.4 0.1 iota_compare_fusion
  2.4 0.1 iota_compare_fusion.1
  2.5 0.1 broadcast_and_fusion
  2.6 0.8 select_reduce_fusion.asked
  3.4 156.5 %shard_map.46 = (bf16[384,2048]{1,0:T(8,128)(2,1)}, bf16[384,1024]{1,0:T(8,128)(2,1)}, bf16[384,1024]{1,0:T(8,128)(2,1)}) custom-call(s32[8,12]{1,0:T(8,128)} %bitcast.7, s32[3,12]{1,0:T(4,128)} %fusion.5.slots_of, s32[7,8,128]{2,1,0:T(8,128)} %select_reduce_fusion.asked, bf16[384,4096]{1,0:T(8,128)(2,1)} %queries.1, bf16[64,128,256]{2,1,0:T(8,128)(2,1)} %bitcast.3, ...), custom_call_target="tpu_custom_call" | custom-call | tf_op jit(solution)/shard_map/pallas_call | solution.py:422
  159.9 5.5 %shard_map.47 = bf16[384,4096]{1,0:T(8,128)(2,1)} custom-call(bf16[384,2048]{1,0:T(8,128)(2,1)} %get-tuple-element.8.refs_0_, bf16[384,1024]{1,0:T(8,128)(2,1)} %get-tuple-element.9.refs_1_, bf16[384,1024]{1,0:T(8,128)(2,1)} %get-tuple-element.10.refs_2_), custom_call_target="tpu_custom_call" | custom-call | tf_op jit(solution)/shard_map/pallas_call | solution.py:459
  (2 shorter events, 0.0 us)
